TPU v7x, 1024 devices: a whole 4x8x16 slice. The times are simulated.
1024 devices in a mesh: dp: 16 (over y, core), expert: 64 (over x, z).
Axes of the slice: x: 4, y: 8, z: 16, core: 2. Of those that a mesh axis runs over, the one named last changes fastest.
Arguments:
- tokens: bfloat16 [8192, 4096], P('expert', 'dp'), may hold values from -6 to 6
- out_grad: bfloat16 [8192, 4096], P('expert', 'dp'), may hold values from -6 to 6
- route_expert: int32 [8192, 2], P('expert'), may hold values from 0 to 63, all different within a row; in each aligned block of 128 rows (0 to 127, 128 to 255, ...) at most 8 rows name the same one
- route_weight: float32 [8192, 2], P('expert'), may hold values from 0.1 to 1
- gate_weight: bfloat16 [64, 4096, 768], P('expert', 'dp'), may hold values from -0.09375 to 0.09375
- up_weight: bfloat16 [64, 4096, 768], P('expert', 'dp'), may hold values from -0.09375 to 0.09375
- down_weight: bfloat16 [64, 768, 4096], P('expert', None, 'dp'), may hold values from -0.21875 to 0.21875
Outputs:
- grad_tokens: float32 [8192, 4096], P('expert', 'dp')
- grad_gate: bfloat16 [64, 4096, 768], P('expert', 'dp')
- grad_up: bfloat16 [64, 4096, 768], P('expert', 'dp')
- grad_down: bfloat16 [64, 768, 4096], P('expert', None, 'dp')
Inputs may be any that keep to these rules, and one draw needn't show every extreme that they name: `route_expert`: each token's 2 experts differ; among the tokens of one index of the expert axis (aligned blocks of 128 tokens) no expert is named by more than 8 routes, a bound that some block reaches.
All inputs are finite; a program needn't handle non-finite values.
Results may differ from a plain program's by a relative error of at most 0.0057.
Values may be sent and summed in bfloat16 or wider, within the bound.
A program may use at most 32 MiB of HBM per device.

v0:
```python
import jax
import jax.numpy as jnp
from jax import lax
from jax.sharding import PartitionSpec as P


def contract(left, right, left_dim, right_dim):
    return lax.dot_general(
        left, right, (((left_dim,), (right_dim,)), ((), ())), preferred_element_type=jnp.float32
    )


def local(tokens, out_grad, route_expert, route_weight, gate_weight, up_weight, down_weight):
    tok_rows, width_local = tokens.shape
    top_count = route_expert.shape[1]
    experts_all = lax.axis_size("expert")
    capacity = 2 * tok_rows * top_count // experts_all
    route_count = tok_rows * top_count
    slots = experts_all * capacity
    flat_expert = route_expert.reshape(route_count)
    route_order = jnp.arange(route_count, dtype=jnp.int32)
    earlier_same = (flat_expert[:, None] == flat_expert[None, :]) & (
        route_order[None, :] < route_order[:, None]
    )
    slot_rank = jnp.sum(earlier_same.astype(jnp.int32), axis=1)
    position = flat_expert * capacity + slot_rank
    token_of = route_order // top_count
    x_rows = tokens[token_of]
    scaled = (
        route_weight.reshape(route_count)[:, None] * out_grad[token_of].astype(jnp.float32)
    ).astype(jnp.bfloat16)
    send_x = jnp.zeros((slots, width_local), jnp.bfloat16).at[position].set(x_rows)
    send_g = jnp.zeros((slots, width_local), jnp.bfloat16).at[position].set(scaled)
    recv_x, recv_g = (
        lax.all_to_all(send_x, "expert", split_axis=0, concat_axis=0, tiled=True),
        lax.all_to_all(send_g, "expert", split_axis=0, concat_axis=0, tiled=True),
    )
    w_gate = gate_weight[0]
    w_up = up_weight[0]
    w_down = down_weight[0]
    hidden = w_gate.shape[1]
    pre_sums = lax.psum_scatter(
        jnp.concatenate(
            [
                jnp.dot(recv_x, w_gate, preferred_element_type=jnp.float32),
                jnp.dot(recv_x, w_up, preferred_element_type=jnp.float32),
            ],
            axis=1,
        ),
        "dp",
        scatter_dimension=0,
        tiled=True,
    )
    d_act = lax.psum_scatter(contract(recv_g, w_down, 1, 1), "dp", scatter_dimension=0, tiled=True)
    gate = pre_sums[:, :hidden]
    upper = pre_sums[:, hidden:]
    sigma = jax.nn.sigmoid(gate)
    silu_value = gate * sigma
    activation = (silu_value * upper).astype(jnp.bfloat16)
    d_gate = (d_act * upper * sigma * (1.0 + gate * (1.0 - sigma))).astype(jnp.bfloat16)
    d_up = (d_act * silu_value).astype(jnp.bfloat16)
    act_all, gate_all, up_all = (
        lax.all_gather(activation, "dp", axis=0, tiled=True),
        lax.all_gather(d_gate, "dp", axis=0, tiled=True),
        lax.all_gather(d_up, "dp", axis=0, tiled=True),
    )
    grad_down = contract(act_all, recv_g, 0, 0)
    grad_gate = contract(recv_x, gate_all, 0, 0)
    grad_up = contract(recv_x, up_all, 0, 0)
    d_rows = contract(gate_all, w_gate, 1, 1) + contract(up_all, w_up, 1, 1)
    returned = lax.all_to_all(
        d_rows.astype(jnp.bfloat16), "expert", split_axis=0, concat_axis=0, tiled=True
    )
    route_grads = returned[position].astype(jnp.float32).reshape(tok_rows, top_count, width_local)
    grad_tokens = jnp.sum(route_grads, axis=1)
    return (
        grad_tokens,
        grad_gate.astype(jnp.bfloat16)[None],
        grad_up.astype(jnp.bfloat16)[None],
        grad_down.astype(jnp.bfloat16)[None],
    )


def solution(mesh):
    in_specs = (
        P("expert", "dp"),
        P("expert", "dp"),
        P("expert", None),
        P("expert", None),
        P("expert", "dp", None),
        P("expert", "dp", None),
        P("expert", None, "dp"),
    )
    out_specs = (
        P("expert", "dp"),
        P("expert", "dp", None),
        P("expert", "dp", None),
        P("expert", None, "dp"),
    )
    return jax.shard_map(local, mesh=mesh, in_specs=in_specs, out_specs=out_specs, check_vma=False)
```

profile of v0, /device:TPU:1, one launch (start us, length us, event | category | flops | bytes accessed | tf_op | source)
XLA Modules:
  0.0 273.2 jit_solution(17407970443617559298)
XLA Ops:
  7.2 0.8 copy.15
  8.1 0.7 broadcast_multiply_fusion
  8.7 0.1 eq.15
  8.9 0.2 convert_reduce_fusion
  9.1 0.1 copy.14
  9.2 0.1 mul.49
  9.3 0.8 copy.16
  10.1 0.1 mul.50
  10.3 3.7 %scatter_custom_fusion = bf16[512,256]{1,0:T(8,128)(2,1)S(1)} fusion(s32[256]{0:T(256)S(1)} %bitcast.49, f32[256]{0:T(256)S(1)} %mul.50, bf16[]{:T(256)} %constant.10.clone.1, bf16[128,256]{1,0:T(8,128)(2,1)} %param.8, s32[1024]{0:T(1024)S(1)} %pad_clamp_fusion.1), kind=kCustom, calls=%fused_computation.34 | custom fusion | flops 196608 | bytes 332802 | tf_op jit(solution)/shard_map/scatter | solution.py:33
  13.9 41.6 %all_to_all.36 = bf16[64,8,256]{2,1,0:T(8,128)(2,1)S(1)} all-to-all(bf16[64,8,256]{2,1,0:T(8,128)(2,1)S(1)} %bitcast.48), channel_id=1, replica_groups=mesh['dp'=16,'expert'=64] {'expert'}, dimensions={0} | all-to-all | bytes 524288 | tf_op jit(solution)/shard_map/all_to_all | solution.py:36
  55.6 2.5 fusion.12
  58.2 0.0 reduce-scatter.5.cloned.1.call-start
  58.2 3.6 %scatter_custom_fusion.1 = bf16[512,256]{1,0:T(8,128)(2,1)S(1)} fusion(s32[256]{0:T(256)S(1)} %bitcast.50, bf16[128,256]{1,0:T(8,128)(2,1)} %param.7, s32[1024]{0:T(1024)S(1)} %pad_clamp_fusion.1, bf16[]{:T(256)} %constant.10.clone.1), kind=kCustom, calls=%fused_computation.35 | custom fusion | bytes 262656 | tf_op jit(solution)/shard_map/scatter | solution.py:32
  61.8 25.5 %all_to_all.37 = bf16[64,8,256]{2,1,0:T(8,128)(2,1)S(1)} all-to-all(bf16[64,8,256]{2,1,0:T(8,128)(2,1)S(1)} %bitcast.47), channel_id=1, replica_groups=mesh['dp'=16,'expert'=64] {'expert'}, dimensions={0} | all-to-all | bytes 524288 | tf_op jit(solution)/shard_map/all_to_all | solution.py:35
  87.3 0.4 fusion.10
  87.7 0.4 fusion.6
  88.1 2.0 pad_maximum_fusion
  90.2 28.7 %reduce-scatter.3.cloned.1.call-done = f32[32,768]{1,0:T(8,128)} async-done(((f32[512,768]{1,0:T(8,128)}), f32[32,768]{1,0:T(8,128)}) %reduce-scatter.3.cloned.1.call-update) | async-done | bytes 98320 | tf_op jit(solution)/shard_map/reduce_scatter | solution.py:54
  118.8 71.0 %reduce-scatter.5.cloned.1.call-done = f32[32,1536]{1,0:T(8,128)} async-done(((f32[512,1536]{1,0:T(8,128)}), f32[32,1536]{1,0:T(8,128)}) %reduce-scatter.5.cloned.1.call-update) | async-done | bytes 196624 | tf_op jit(solution)/shard_map/reduce_scatter | solution.py:42
  189.8 1.0 multiply_convert_fusion.3
  190.9 17.5 %all_gather.9 = bf16[512,768]{1,0:T(8,128)(2,1)S(1)} all-gather(bf16[32,768]{1,0:T(8,128)(2,1)S(1)} %get-tuple-element.5), channel_id=1, replica_groups=mesh['dp'=16,'expert'=64] {'dp'}, dimensions={0}, use_global_device_ids=true | all-gather | bytes 835584 | tf_op jit(solution)/shard_map/all_gather | solution.py:64
  208.3 0.4 fusion.8
  208.8 18.1 %all_gather.10 = bf16[512,768]{1,0:T(8,128)(2,1)S(1)} all-gather(bf16[32,768]{1,0:T(8,128)(2,1)S(1)} %get-tuple-element.4), channel_id=1, replica_groups=mesh['dp'=16,'expert'=64] {'dp'}, dimensions={0}, use_global_device_ids=true | all-gather | bytes 835584 | tf_op jit(solution)/shard_map/all_gather | solution.py:65
  226.8 1.1 fusion.4
  227.9 15.9 %all-to-all-start.2 = ((bf16[64,8,256]{2,1,0:T(8,128)(2,1)}), bf16[64,8,256]{2,1,0:T(8,128)(2,1)S(1)}, u32[]{:S(2)}, u32[]{:S(2)}) async-start(bf16[64,8,256]{2,1,0:T(8,128)(2,1)} %fusion.4), calls=%async_computation.4 | async-start | bytes 524288 | tf_op jit(solution)/shard_map/all_to_all | solution.py:71
  243.8 1.1 fusion.1
  244.9 1.1 fusion.2
  246.1 16.9 %all_gather.11 = bf16[512,768]{1,0:T(8,128)(2,1)S(1)} all-gather(bf16[32,768]{1,0:T(8,128)(2,1)S(1)} %get-tuple-element.6), channel_id=1, replica_groups=mesh['dp'=16,'expert'=64] {'dp'}, dimensions={0}, use_global_device_ids=true | all-gather | bytes 835584 | tf_op jit(solution)/shard_map/all_gather | solution.py:63
  263.0 1.2 fusion.3
  264.1 1.2 gather_fusion
  265.3 0.1 reshape.93
  265.4 1.0 reduce_sum.22
  (12 shorter events, 0.1 us)
Async XLA Ops:
  7.2 80.2 %copy-start = (bf16[1,256,768]{2,1,0:T(8,128)(2,1)S(1)}, bf16[1,256,768]{2,1,0:T(8,128)(2,1)}, u32[]{:S(2)}) copy-start(bf16[1,256,768]{2,1,0:T(8,128)(2,1)} %param.11) | copy-start | bytes 1179652
  7.2 111.6 %reduce-scatter.3.cloned.1.call-start = ((), (), s32[]{:S(2)}) async-start(), calls=%async_computation.5 | async-start | bytes 1671168 | tf_op jit(solution)/shard_map/reduce_scatter | solution.py:54
  58.2 29.5 %copy-start.1 = (bf16[1,256,768]{2,1,0:T(8,128)(2,1)S(1)}, bf16[1,256,768]{2,1,0:T(8,128)(2,1)}, u32[]{:S(2)}) copy-start(bf16[1,256,768]{2,1,0:T(8,128)(2,1)} %param.12) | copy-start | bytes 1179652
  58.2 131.6 %reduce-scatter.5.cloned.1.call-start = ((), (), s32[]{:S(2)}) async-start(), calls=%async_computation.6 | async-start | bytes 3342336 | tf_op jit(solution)/shard_map/reduce_scatter | solution.py:42
  227.9 36.2 %all-to-all-start.2 = ((bf16[64,8,256]{2,1,0:T(8,128)(2,1)}), bf16[64,8,256]{2,1,0:T(8,128)(2,1)S(1)}, u32[]{:S(2)}, u32[]{:S(2)}) async-start(bf16[64,8,256]{2,1,0:T(8,128)(2,1)} %fusion.4), calls=%async_computation.4 | async-start | bytes 524288 | tf_op jit(solution)/shard_map/all_to_all | solution.py:71
Sparse Core Ops, SparseCore 0:
  58.3 60.4 reduce-scatter.2
  122.6 67.1 reduce-scatter.4
where the time goes:
time: 274 us; the launch traced here: 273 us
  blocking collectives  120 us (44%)
  waiting for transfers between devices  99.7 us (36%)
  starting transfers between devices  15.9 us (6%)
  between operations  14.1 us (5%)
  other arithmetic  8.6 us (3%)
  matrix products  8.22 us (3%)
  local copies, waits for them, and re-layouts  7.01 us (3%)
    reduce_scatter x1, waiting for transfers between devices, local(): lax.psum_scatter(jnp.concatenate([jnp.dot(recv_x, w_gate, preferred_eleme...  71 us
    all_to_all x1, blocking collectives, local(): lax.all_to_all(send_g, 'expert', split_axis=0, concat_axis=0, tiled=True)  41.6 us
    reduce_scatter x1, waiting for transfers between devices, local(): lax.psum_scatter(contract(recv_g, w_down, 1, 1), 'dp', scatter_dimension=...  28.7 us
    all_to_all x1, blocking collectives, local(): lax.all_to_all(send_x, 'expert', split_axis=0, concat_axis=0, tiled=True)  25.5 us
    all_gather x1, blocking collectives, local(): lax.all_gather(d_up, 'dp', axis=0, tiled=True)  18.1 us
    all_gather x1, blocking collectives, local(): lax.all_gather(d_gate, 'dp', axis=0, tiled=True)  17.5 us
    all_gather x1, blocking collectives, local(): lax.all_gather(activation, 'dp', axis=0, tiled=True)  16.9 us
    all_to_all x1, starting transfers between devices, local(): lax.all_to_all(d_rows.astype(jnp.bfloat16), 'expert', split_axis=0, conca...  15.9 us
  transfers between devices with their start and end apart: 3, of which 2 were waited for; matrix products, arithmetic and copies ran while one was open for 4% of the time, Pallas kernels for 0%

commit v1 on v0

v1 whole, which is shorter than its diff:
```python
import functools

import jax
import jax.numpy as jnp
from jax import lax
from jax.experimental import pallas as pl
from jax.experimental.pallas import tpu as pltpu
from jax.sharding import PartitionSpec as P

MESH = pl.DeviceIdType.MESH
NX, NZ, NY = 4, 16, 8
EXPERTS = NX * NZ
TOK, FEAT, HID, CAP = 128, 256, 768, 8
HALF = HID // 2
CHUNKS = 8
SRC = EXPERTS // 2 // CHUNKS
ROWS = SRC * CAP
MINE = CHUNKS * ROWS
LONG, SHORT = NY // 2, NY // 2 - 1
DZ = ((1, 15), (2, 14), (7, 9), (6, 10), (0, 8), (5, 11), (4, 12), (3, 13))
DIRECT = (7,)
DEPTH = 3
ARRIVE = (5, 9, 16, 20, 24, 26, 28, 30)
TWO_STEPS = dict(D=0, B=4.7, F=9.5, H=14.5, E=19)
ONE_STEP = dict(D=0, F=6.5, E=13)
ORDER = sorted(
    (ARRIVE[k] + after, k, name)
    for k in range(CHUNKS)
    for name, after in (ONE_STEP if k in DIRECT else TWO_STEPS).items()
)
VMEM_LIMIT = 60 * 1024 * 1024
F32, BF16 = jnp.float32, jnp.bfloat16


def dot(a, b, ca, cb):
    return lax.dot_general(a, b, (((ca,), (cb,)), ((), ())), preferred_element_type=F32)


def kernel(
    tok_hbm, og_hbm, rexp_hbm, rwt_hbm, wg, wu, wd,
    g_tok_hbm, g_gate_hbm, g_up_hbm, g_down_hbm,
    tok, og, rexp, rwt, g_tok, g_gate, g_up, g_down,
    wgu, wdn, send, qt, rx, xs, part, out_blocks, in_blocks, dall, rsend, ret, xall, gall,
    a_sem, o_sem, w_sem, ws_send, ws_recv, d_send, d_recv, x_send, x_recv,
    rs_send, rs_recv, ag_send, ag_recv, sh_send, sh_recv, r_send, r_recv,
):
    dp, ex = lax.axis_index("dp"), lax.axis_index("expert")
    y, c = lax.div(dp, 2), lax.rem(dp, 2)
    x, z = lax.div(ex, NZ), lax.rem(ex, NZ)
    sib = (y * 2 + 1 - c, ex)
    sigma = 1 - 2 * c

    small = [
        pltpu.make_async_copy(s, d, a_sem.at[i])
        for i, (s, d) in enumerate([(rexp_hbm, rexp), (rwt_hbm, rwt), (tok_hbm, tok), (og_hbm, og)])
    ]
    for copy in small:
        copy.start()

    x_at = [lax.rem(x + dx, NX) * NZ for dx in range(NX)]
    z_at = [lax.rem(z + dz, NZ) for dz in range(NZ)]
    y_at = {n: lax.rem(y + n * sigma + NY, NY) for n in range(-SHORT, LONG + 1)}
    x_even = [lax.rem(x + c + 2 * i, NX) * NZ for i in range(2)]
    x_odd = [lax.rem(x + 1 - c + 2 * i, NX) * NZ for i in range(2)]
    x_back = [lax.rem(x + 2 * NX - c - 2 * i, NX) * NZ for i in range(2)]

    def along_y(n):
        return (y_at[n] * 2 + c, ex)

    barrier = pltpu.get_barrier_semaphore()

    def signal(target):
        pl.semaphore_signal(barrier, inc=1, device_id=target, device_id_type=MESH)

    for dz in [8, 7, 9, 6, 10, 5, 11, 4, 12, 3, 13, 2, 14, 1, 15, 0]:
        for i in range(2):
            if dz == 0 and i == 0:
                pl.when(c == 1)(lambda: signal((y * 2, x_even[0] + z_at[0])))
            else:
                signal((y * 2, x_even[i] + z_at[dz]))
            signal((y * 2 + 1, x_even[i] + z_at[dz]))
            signal((y * 2 + 1 - c, x_odd[i] + z_at[dz]))
    for n in (4, 3, -3, 2, -2, 1, -1):
        signal(along_y(n))

    own_cols = pl.ds(pl.multiple_of(c * FEAT, FEAT), FEAT)
    sib_cols = pl.ds(pl.multiple_of((1 - c) * FEAT, FEAT), FEAT)

    def weight_parts():
        for hh in range(2):
            h_cols = pl.ds(hh * HALF, HALF)
            yield wg.at[0, :, h_cols], wgu.at[hh, own_cols, pl.ds(0, HALF)]
            yield wu.at[0, :, h_cols], wgu.at[hh, own_cols, pl.ds(HALF, HALF)]
        yield wd.at[0], wdn.at[:, own_cols]

    w_local = [pltpu.make_async_copy(s, d, w_sem.at[i]) for i, (s, d) in enumerate(weight_parts())]
    for copy in w_local:
        copy.start()
    for copy in small:
        copy.wait()

    lane = lax.broadcasted_iota(jnp.int32, (TOK, TOK), 1)
    sub = lax.broadcasted_iota(jnp.int32, (TOK, TOK), 0)
    ef, w = rexp[...].astype(F32), rwt[...]
    e0r, e1r = ef[0:1, :], ef[1:2, :]
    columns = jnp.where(
        sub == 0, e0r, jnp.where(sub == 1, e1r, jnp.where(sub == 2, w[0:1, :], w[1:2, :]))
    ).T
    e0c, e1c, w0c, w1c = columns[:, 0:1], columns[:, 1:2], columns[:, 2:3], columns[:, 3:4]
    slots = 2 * EXPERTS * CAP
    si = lax.broadcasted_iota(jnp.int32, (slots, TOK), 0)
    s_exp = (si // (2 * CAP)).astype(F32)
    s_rank = (si % CAP).astype(F32)
    s_cot = (si % (2 * CAP)) >= CAP
    m0 = (s_exp == e0r).astype(F32)
    m1 = (s_exp == e1r).astype(F32)
    rank = dot((m0 + m1).astype(BF16), (sub < lane).astype(BF16), 1, 0)
    hit = rank == s_rank
    zero = jnp.zeros_like(m0)
    p0 = jnp.where(hit, m0, zero)
    p1 = jnp.where(hit, m1, zero)
    onehot = jnp.concatenate(
        [jnp.where(s_cot, zero, p0 + p1), jnp.where(s_cot, p0, zero), jnp.where(s_cot, p1, zero)], axis=1
    ).astype(BF16)
    o = og[...].astype(F32)
    g0 = (w0c * o).astype(BF16)
    g1 = (w1c * o).astype(BF16)
    values = jnp.concatenate([tok[...], g0, g1], axis=0)
    send[...] = dot(onehot, values, 1, 0).astype(BF16)

    pl.semaphore_wait(barrier, 102 + c)

    def dispatch(k):
        for j, dz in enumerate(DZ[k]):
            for dx in range(NX):
                target = x_at[dx] + z_at[dz]
                src = send.at[pl.ds(pl.multiple_of(target * 16, 16), 16), :]
                dst = rx.at[k, pl.ds((j * 2 + dx // 2) * 16, 16), own_cols]
                copy = pltpu.make_async_remote_copy(
                    src, dst, d_send, d_recv.at[k],
                    device_id=(y * 2 + dx % 2, target), device_id_type=MESH,
                )
                if dx == 0 and dz == 0:
                    pl.when(c == 0)(pltpu.make_async_copy(src, dst, d_recv.at[k]).start)
                    pl.when(c == 1)(copy.start)
                else:
                    copy.start()

    dispatch(0)
    w_remote = [
        pltpu.make_async_remote_copy(
            s, d, ws_send.at[i], ws_recv.at[i], device_id=sib, device_id_type=MESH
        )
        for i, (s, d) in enumerate(weight_parts())
    ]
    for copy in w_remote:
        copy.start()
    for k in range(1, DEPTH):
        dispatch(k)

    ti = lax.broadcasted_iota(jnp.int32, (TOK, slots), 1)
    t_exp = (ti // (2 * CAP)).astype(F32)
    t_rank = (ti % CAP).astype(F32)
    t_cot = (ti % (2 * CAP)) >= CAP
    tm = (t_exp == e0c).astype(F32) + (t_exp == e1c).astype(F32)
    trank = dot((lane < sub).astype(BF16), tm.astype(BF16), 1, 0)
    tz = jnp.zeros_like(tm)
    tp = jnp.where(trank == t_rank, tm, tz)
    qt[0:TOK, :] = jnp.where(t_cot, tz, tp).astype(BF16)
    qt[TOK:, :] = jnp.where(t_cot, tp, tz).astype(BF16)

    for copy in w_local:
        copy.wait()

    def whole(ref, sem):
        pltpu.make_async_copy(ref, ref, sem).wait()

    def split(rows16):
        v = rows16.astype(F32)
        width = v.shape[1]
        v = v.reshape(SRC, 2, CAP, width)
        return v[:, 0].reshape(ROWS, width).astype(BF16), v[:, 1].reshape(ROWS, width).astype(BF16)

    def rows_of(blocks):
        return blocks.astype(F32).reshape(blocks.shape[0] * CAP, blocks.shape[2]).astype(BF16)

    RS_TO = [2, 1, -1, 1, -1, 2, -2]
    RS_FOR = [4, 3, -3, 1, -1, 2, -2]
    RS_ADD = {5: (0, 1), 6: (2,)}
    FAR_FIRST = [4, 3, -3, 2, -2, 1, -1]

    def block(k, n):
        return part[k, pl.ds(pl.multiple_of(y_at[n] * 8, 8), 8), :]

    def rs(k, m):
        return pltpu.make_async_remote_copy(
            out_blocks.at[k, m], in_blocks.at[k, m], rs_send, rs_recv.at[k, m],
            device_id=along_y((FAR_FIRST if k in DIRECT else RS_TO)[m]), device_id_type=MESH,
        )

    AG_TO = [2, -2, 1, -1, 1, 2, -1]
    AG_OF = [0, 0, 0, 0, -2, -2, 2]

    def home(k, n):
        who = y_at[n]
        return dall.at[lax.div(who, 4), (c * CHUNKS + k) * 4 + lax.rem(who, 4)]

    def ag(k, m):
        ref = home(k, 0 if k in DIRECT else AG_OF[m])
        to = along_y((FAR_FIRST if k in DIRECT else AG_TO)[m])
        return pltpu.make_async_remote_copy(
            ref, ref, ag_send, ag_recv.at[k, m], device_id=to, device_id_type=MESH
        )

    def x_share(k):
        return pltpu.make_async_remote_copy(
            rx.at[k, :, sib_cols], xs.at[k], x_send, x_recv.at[k], device_id=sib, device_id_type=MESH
        )

    def own_rows(k):
        return pl.ds(pl.multiple_of(c * MINE + k * ROWS, ROWS), ROWS)

    def sib_rows(k):
        return pl.ds(pl.multiple_of((1 - c) * MINE + k * ROWS, ROWS), ROWS)

    def own_blocks(k):
        return pl.ds((c * CHUNKS + k) * 4, 4)

    def d_share(k):
        ref = dall.at[:, own_blocks(k)]
        return pltpu.make_async_remote_copy(
            ref, ref, sh_send, sh_recv.at[k], device_id=sib, device_id_type=MESH
        )

    def stage_first(k):
        whole(rx.at[k], d_recv.at[k])
        if k + DEPTH < CHUNKS:
            dispatch(k + DEPTH)
        x_share(k).start()
        if k == 0:
            for copy in w_remote:
                copy.wait_recv()
        xv, gv = split(rx[k])
        for hh in range(2):
            part[k, hh * ROWS:(hh + 1) * ROWS, 0:HID] = dot(xv, wgu[hh], 1, 0)
            part[k, hh * ROWS:(hh + 1) * ROWS, HID:] = dot(gv, wdn[hh * HALF:(hh + 1) * HALF, :], 1, 1)
        for m in range(7 if k in DIRECT else 5):
            out_blocks[k, m] = block(k, (FAR_FIRST if k in DIRECT else RS_FOR)[m]).astype(BF16)
            rs(k, m).start()

    def stage_relay(k):
        for m in (5, 6):
            acc = block(k, RS_FOR[m])
            for n in RS_ADD[m]:
                rs(k, n).wait_recv()
                acc = acc + in_blocks[k, n].astype(F32)
            out_blocks[k, m] = acc.astype(BF16)
            rs(k, m).start()

    def stage_point(k):
        acc = block(k, 0)
        for m in range(0 if k in DIRECT else 3, 7):
            rs(k, m).wait_recv()
            acc = acc + in_blocks[k, m].astype(F32)
        gate, upper, d_act = acc[:, 0:HALF], acc[:, HALF:HID], acc[:, HID:]
        sigma_v = jax.nn.sigmoid(gate)
        silu = gate * sigma_v
        home(k, 0)[:, 0:HALF] = (d_act * upper * sigma_v * (1.0 + gate * (1.0 - sigma_v))).astype(BF16)
        home(k, 0)[:, HALF:HID] = (d_act * silu).astype(BF16)
        home(k, 0)[:, HID:] = (silu * upper).astype(BF16)
        for m in range(7 if k in DIRECT else 4):
            ag(k, m).start()

    def stage_forward(k):
        ag(k, 0).wait_recv()
        ag(k, 4).start()
        ag(k, 5).start()
        ag(k, 1).wait_recv()
        ag(k, 6).start()

    def stage_back(k):
        for m in range(0 if k in DIRECT else 2, 7):
            ag(k, m).wait_recv()
        d_share(k).start()
        rows_grad = dot(rows_of(dall[0, own_blocks(k), :, 0:HID]), wgu[0], 1, 1)
        rows_grad = rows_grad + dot(rows_of(dall[1, own_blocks(k), :, 0:HID]), wgu[1], 1, 1)
        rg = rows_grad.reshape(SRC, CAP, 2 * FEAT)
        for cc in range(2):
            lo = cc * FEAT
            rsend[k, cc] = (
                jnp.concatenate([rg[:, :, lo:lo + 128], rg[:, :, lo + 128:lo + 256]], axis=1)
                .reshape(SRC * 16, 128).astype(BF16)
            )
        dst = ret.at[pl.ds(pl.multiple_of(ex * 16, 16), 16), :]
        for j, dz in enumerate(DZ[k]):
            for i in range(2):
                target = x_back[i] + z_at[(NZ - dz) % NZ]
                for cc in range(2):
                    src = rsend.at[k, cc, pl.ds((j * 2 + i) * 16, 16), :]
                    copy = pltpu.make_async_remote_copy(
                        src, dst, r_send, r_recv, device_id=(y * 2 + cc, target), device_id_type=MESH
                    )
                    if dz == 0 and i == 0 and cc == 0:
                        pl.when(c == 0)(pltpu.make_async_copy(src, dst, r_recv).start)
                        pl.when(c == 1)(copy.start)
                    else:
                        copy.start()

    stages = dict(D=stage_first, B=stage_relay, F=stage_point, H=stage_forward, E=stage_back)
    for _, k, name in ORDER:
        stages[name](k)

    for k in range(CHUNKS):
        x_share(k).wait_recv()
        xv, gv = split(rx[k, :, own_cols])
        xall[own_rows(k), :] = xv
        gall[own_rows(k), :] = gv
        xv, gv = split(xs[k])
        xall[sib_rows(k), :] = xv
        gall[sib_rows(k), :] = gv
    for k in range(CHUNKS):
        whole(dall.at[:, pl.ds(((1 - c) * CHUNKS + k) * 4, 4)], sh_recv.at[k])
    for hh in range(2):
        grads = rows_of(dall[hh])
        gu = dot(xall[...], grads[:, 0:HID], 0, 0).astype(BF16)
        g_gate[0, :, hh * HALF:(hh + 1) * HALF] = gu[:, 0:HALF]
        g_up[0, :, hh * HALF:(hh + 1) * HALF] = gu[:, HALF:]
        g_down[0, hh * HALF:(hh + 1) * HALF, :] = dot(grads[:, HID:], gall[...], 0, 0).astype(BF16)
    results = [
        pltpu.make_async_copy(v, h, o_sem.at[i])
        for i, (v, h) in enumerate(
            [(g_gate, g_gate_hbm), (g_up, g_up_hbm), (g_down, g_down_hbm), (g_tok, g_tok_hbm)]
        )
    ]
    for copy in results[:3]:
        copy.start()

    whole(ret, r_recv)
    both = dot(qt[...], ret[...], 1, 0)
    g_tok[:, 0:128] = both[0:TOK]
    g_tok[:, 128:] = both[TOK:]
    results[3].start()

    for copy in w_remote:
        copy.wait_send()
    whole(out_blocks, rs_send)
    whole(out_blocks, ag_send)
    whole(xs, x_send)
    whole(dall.at[:, pl.ds(0, 4 * CHUNKS)], sh_send)
    for source, sem in ((send, d_send), (ret, r_send)):
        pl.when(c == 0)(functools.partial(whole, source.at[pl.ds(0, EXPERTS * 16 - 16), :], sem))
        pl.when(c == 1)(functools.partial(whole, source, sem))
    for copy in results:
        copy.wait()


def hand_out(*refs):
    into, out = refs[12], refs[13]
    reads = [pltpu.make_async_copy(refs[i], refs[8 + i], into.at[i]) for i in range(4)]
    writes = [pltpu.make_async_copy(refs[8 + i], refs[4 + i], out.at[i]) for i in range(4)]
    for copy in reads:
        copy.start()
    for read, write in zip(reads, writes):
        read.wait()
        write.start()
    for copy in writes:
        copy.wait()


def local(tokens, out_grad, route_expert, route_weight, *weights):
    hbm = pl.BlockSpec(memory_space=pl.ANY)
    dma = pltpu.SemaphoreType.DMA
    shapes = (
        jax.ShapeDtypeStruct((TOK, FEAT), F32),
        jax.ShapeDtypeStruct((1, FEAT, HID), BF16),
        jax.ShapeDtypeStruct((1, FEAT, HID), BF16),
        jax.ShapeDtypeStruct((1, HID, FEAT), BF16),
    )
    found = pl.pallas_call(
        kernel,
        out_shape=shapes,
        in_specs=[hbm] * 7,
        out_specs=[hbm] * 4,
        scratch_shapes=[
            pltpu.VMEM((TOK, FEAT), BF16),
            pltpu.VMEM((TOK, FEAT), BF16),
            pltpu.VMEM((2, TOK), jnp.int32),
            pltpu.VMEM((2, TOK), F32),
            pltpu.VMEM((TOK, FEAT), F32),
            pltpu.VMEM((1, FEAT, HID), BF16),
            pltpu.VMEM((1, FEAT, HID), BF16),
            pltpu.VMEM((1, HID, FEAT), BF16),
            pltpu.VMEM((2, 2 * FEAT, HID), BF16),
            pltpu.VMEM((HID, 2 * FEAT), BF16),
            pltpu.VMEM((EXPERTS * 16, FEAT), BF16),
            pltpu.VMEM((2 * TOK, EXPERTS * 16), BF16),
            pltpu.VMEM((CHUNKS, SRC * 16, 2 * FEAT), BF16),
            pltpu.VMEM((CHUNKS, SRC * 16, FEAT), BF16),
            pltpu.VMEM((CHUNKS, 2 * ROWS, 3 * HALF), F32),
            pltpu.VMEM((CHUNKS, 7, 8, 3 * HALF), BF16),
            pltpu.VMEM((CHUNKS, 7, 8, 3 * HALF), BF16),
            pltpu.VMEM((2, 8 * CHUNKS, CAP, 3 * HALF), BF16),
            pltpu.VMEM((CHUNKS, 2, SRC * 16, 128), BF16),
            pltpu.VMEM((EXPERTS * 16, 128), BF16),
            pltpu.VMEM((2 * MINE, FEAT), BF16),
            pltpu.VMEM((2 * MINE, FEAT), BF16),
            dma((4,)), dma((4,)), dma((5,)), dma((5,)), dma((5,)),
            dma, dma((CHUNKS,)), dma, dma((CHUNKS,)),
            dma, dma((CHUNKS, 7)), dma, dma((CHUNKS, 7)),
            dma, dma((CHUNKS,)), dma, dma,
        ],
        compiler_params=pltpu.CompilerParams(
            collective_id=0, has_side_effects=True, vmem_limit_bytes=VMEM_LIMIT
        ),
        name="expert_backward",
    )(tokens, out_grad, route_expert.T, route_weight.T, *weights)
    return pl.pallas_call(
        hand_out,
        out_shape=shapes,
        in_specs=[hbm] * 4,
        out_specs=[hbm] * 4,
        scratch_shapes=[pltpu.VMEM(a.shape, a.dtype) for a in shapes] + [dma((4,)), dma((4,))],
        name="hand_out",
    )(*found)


def solution(mesh):
    in_specs = (
        P("expert", "dp"),
        P("expert", "dp"),
        P("expert", None),
        P("expert", None),
        P("expert", "dp", None),
        P("expert", "dp", None),
        P("expert", None, "dp"),
    )
    out_specs = (
        P("expert", "dp"),
        P("expert", "dp", None),
        P("expert", "dp", None),
        P("expert", None, "dp"),
    )
    return jax.shard_map(local, mesh=mesh, in_specs=in_specs, out_specs=out_specs, check_vma=False)
```

time: 274 us -> 91.3 us (0.33)
  blocking collectives: 120 us -> 0 us
  waiting for transfers between devices: 99.7 us -> 0 us
  Pallas kernels: 0 us -> 90.4 us
  starting transfers between devices: 15.9 us -> 0 us
  between operations: 14.1 us -> 0.64 us
  other arithmetic: 8.6 us -> 0 us
  matrix products: 8.22 us -> 0 us
  local copies, waits for them, and re-layouts: 7.01 us -> 0 us
    reduce_scatter x2 -> x0, waiting for transfers between devices: 99.7 us -> none  [the longest x1 71 us: local(): lax.psum_scatter(jnp.concatenate([jnp.dot(recv_x, w_gate, preferred_eleme...]
    pallas_call x0 -> x2, Pallas kernels: none -> 90.4 us  [the longest x1 88.3 us: local(): pl.pallas_call(kernel, out_shape=shapes, in_specs=[hbm] * 7, out_specs=[h...]
    all_to_all x2 -> x0, blocking collectives: 67.2 us -> none  [the longest x1 41.6 us: local(): lax.all_to_all(send_g, 'expert', split_axis=0, concat_axis=0, tiled=True)]
    all_gather x3 -> x0, blocking collectives: 52.4 us -> none  [the longest x1 18.1 us: local(): lax.all_gather(d_up, 'dp', axis=0, tiled=True)]
    all_to_all x1 -> x0, starting transfers between devices: 15.9 us -> none  [local(): lax.all_to_all(d_rows.astype(jnp.bfloat16), 'expert', split_axis=0, conca...]
    dot_general x8 -> x0, matrix products: 8.22 us -> none  [the longest x6 7.49 us: contract(): lax.dot_general(left, right, (((left_dim,), (right_dim,)), ((), ())), pre...]
    scatter x1 -> x0, other arithmetic: 3.65 us -> none  [local(): jnp.zeros((slots, width_local), jnp.bfloat16).at[position].set(scaled)]
    scatter x1 -> x0, local copies, waits for them, and re-layouts: 3.57 us -> none  [local(): jnp.zeros((slots, width_local), jnp.bfloat16).at[position].set(x_rows)]
  transfers between devices with their start and end apart: 3 -> 0, of which waited for: 2 -> 0; matrix products, arithmetic and copies ran while one was open for 4% -> 0% of each run, Pallas kernels for 0% -> 0%
where the time goes in v1:
time: 91.3 us; the launch traced here: 91.1 us
  Pallas kernels  90.4 us (99%)
    pallas_call x1, Pallas kernels, local(): pl.pallas_call(kernel, out_shape=shapes, in_specs=[hbm] * 7, out_specs=[h...  88.3 us
    pallas_call x1, Pallas kernels, local(): pl.pallas_call(hand_out, out_shape=shapes, in_specs=[hbm] * 4, out_specs=...  2.14 us

profile of v1, /device:TPU:1, one launch (start us, length us, event | category | flops | bytes accessed | tf_op | source)
XLA Modules:
  0.0 91.1 jit_solution(11640094450649122807)
XLA Ops:
  0.6 88.3 %expert_backward.1 = (f32[128,256]{1,0:T(8,128)}, bf16[1,256,768]{2,1,0:T(8,128)(2,1)}, bf16[1,256,768]{2,1,0:T(8,128)(2,1)}, bf16[1,768,256]{2,1,0:T(8,128)(2,1)}) custom-call(bf16[128,256]{1,0:T(8,128)(2,1)} %tok_hbm.1, bf16[128,256]{1,0:T(8,128)(2,1)} %og_hbm.1, s32[2,128]{1,0:T(2,128)} %bitcast.2, f32[2,128]{1,0:T(2,128)} %bitcast.3, ...), custom_call_target="tpu_custom_call" | custom-call | tf_op jit(solution)/shard_map/expert_backward/pallas_call | solution.py:379
  88.9 2.1 %hand_out.1 = (f32[128,256]{1,0:T(8,128)}, bf16[1,256,768]{2,1,0:T(8,128)(2,1)}, bf16[1,256,768]{2,1,0:T(8,128)(2,1)}, bf16[1,768,256]{2,1,0:T(8,128)(2,1)}) custom-call(f32[128,256]{1,0:T(8,128)} %get-tuple-element.8.refs_0_, bf16[1,256,768]{2,1,0:T(8,128)(2,1)} %get-tuple-element.9.refs_1_, bf16[1,256,768]{2,1,0:T(8,128)(2,1)} %get-tuple-element.10.refs_2_, ...), custom_call_target="tpu_custom_call" | custom-call | tf_op jit(solution)/shard_map/hand_out/pallas_call | solution.py:417

commit v2 on v1

--- a/solution.py
+++ b/solution.py
@@ -17,16 +17,14 @@
 ROWS = SRC * CAP
 MINE = CHUNKS * ROWS
 LONG, SHORT = NY // 2, NY // 2 - 1
-DZ = ((1, 15), (2, 14), (7, 9), (6, 10), (0, 8), (5, 11), (4, 12), (3, 13))
-DIRECT = (7,)
-DEPTH = 3
-ARRIVE = (5, 9, 16, 20, 24, 26, 28, 30)
-TWO_STEPS = dict(D=0, B=4.7, F=9.5, H=14.5, E=19)
-ONE_STEP = dict(D=0, F=6.5, E=13)
-ORDER = sorted(
-    (ARRIVE[k] + after, k, name)
-    for k in range(CHUNKS)
-    for name, after in (ONE_STEP if k in DIRECT else TWO_STEPS).items()
+DZ = ((1, 15), (2, 14), (6, 10), (7, 9), (5, 11), (0, 8), (4, 12), (3, 13))
+DIRECT = ()
+DEPTH = 4
+ORDER = (
+    ("D", 0), ("D", 1), ("B", 0), ("D", 2), ("B", 1), ("F", 0), ("D", 3), ("B", 2), ("F", 1), ("D", 4),
+    ("H", 0), ("B", 3), ("F", 2), ("H", 1), ("D", 5), ("B", 4), ("D", 6), ("F", 3), ("E", 0), ("H", 2),
+    ("D", 7), ("B", 5), ("E", 1), ("F", 4), ("B", 6), ("H", 3), ("B", 7), ("E", 2), ("F", 5), ("H", 4),
+    ("F", 6), ("E", 3), ("F", 7), ("H", 5), ("H", 6), ("E", 4), ("H", 7), ("E", 5), ("E", 6), ("E", 7),
 )
 VMEM_LIMIT = 60 * 1024 * 1024
 F32, BF16 = jnp.float32, jnp.bfloat16
@@ -236,7 +234,6 @@
         whole(rx.at[k], d_recv.at[k])
         if k + DEPTH < CHUNKS:
             dispatch(k + DEPTH)
-        x_share(k).start()
         if k == 0:
             for copy in w_remote:
                 copy.wait_recv()
@@ -247,6 +244,7 @@
         for m in range(7 if k in DIRECT else 5):
             out_blocks[k, m] = block(k, (FAR_FIRST if k in DIRECT else RS_FOR)[m]).astype(BF16)
             rs(k, m).start()
+        x_share(k).start()
 
     def stage_relay(k):
         for m in (5, 6):
@@ -281,7 +279,6 @@
     def stage_back(k):
         for m in range(0 if k in DIRECT else 2, 7):
             ag(k, m).wait_recv()
-        d_share(k).start()
         rows_grad = dot(rows_of(dall[0, own_blocks(k), :, 0:HID]), wgu[0], 1, 1)
         rows_grad = rows_grad + dot(rows_of(dall[1, own_blocks(k), :, 0:HID]), wgu[1], 1, 1)
         rg = rows_grad.reshape(SRC, CAP, 2 * FEAT)
@@ -305,9 +302,10 @@
                         pl.when(c == 1)(copy.start)
                     else:
                         copy.start()
+        d_share(k).start()
 
     stages = dict(D=stage_first, B=stage_relay, F=stage_point, H=stage_forward, E=stage_back)
-    for _, k, name in ORDER:
+    for name, k in ORDER:
         stages[name](k)
 
     for k in range(CHUNKS):

time: 91.3 us -> 89.9 us (0.985)
  Pallas kernels: 90.4 us -> 89.1 us
    pallas_call x1, Pallas kernels: 88.3 us -> 86.9 us  [local(): pl.pallas_call(kernel, out_shape=shapes, in_specs=[hbm] * 7, out_specs=[h...]
where the time goes in v2:
time: 89.9 us; the launch traced here: 89.7 us
  Pallas kernels  89.1 us (99%)
    pallas_call x1, Pallas kernels, local(): pl.pallas_call(kernel, out_shape=shapes, in_specs=[hbm] * 7, out_specs=[h...  86.9 us
    pallas_call x1, Pallas kernels, local(): pl.pallas_call(hand_out, out_shape=shapes, in_specs=[hbm] * 4, out_specs=...  2.14 us

profile of v2, /device:TPU:1, one launch (start us, length us, event | category | flops | bytes accessed | tf_op | source)
XLA Modules:
  0.0 89.7 jit_solution(8408247459602792265)
XLA Ops:
  0.6 86.9 %expert_backward.1 = (f32[128,256]{1,0:T(8,128)}, bf16[1,256,768]{2,1,0:T(8,128)(2,1)}, bf16[1,256,768]{2,1,0:T(8,128)(2,1)}, bf16[1,768,256]{2,1,0:T(8,128)(2,1)}) custom-call(bf16[128,256]{1,0:T(8,128)(2,1)} %tok_hbm.1, bf16[128,256]{1,0:T(8,128)(2,1)} %og_hbm.1, s32[2,128]{1,0:T(2,128)} %bitcast.2, f32[2,128]{1,0:T(2,128)} %bitcast.3, ...), custom_call_target="tpu_custom_call" | custom-call | tf_op jit(solution)/shard_map/expert_backward/pallas_call | solution.py:377
  87.6 2.1 %hand_out.1 = (f32[128,256]{1,0:T(8,128)}, bf16[1,256,768]{2,1,0:T(8,128)(2,1)}, bf16[1,256,768]{2,1,0:T(8,128)(2,1)}, bf16[1,768,256]{2,1,0:T(8,128)(2,1)}) custom-call(f32[128,256]{1,0:T(8,128)} %get-tuple-element.8.refs_0_, bf16[1,256,768]{2,1,0:T(8,128)(2,1)} %get-tuple-element.9.refs_1_, bf16[1,256,768]{2,1,0:T(8,128)(2,1)} %get-tuple-element.10.refs_2_, ...), custom_call_target="tpu_custom_call" | custom-call | tf_op jit(solution)/shard_map/hand_out/pallas_call | solution.py:415
